TPU v7x, 512 devices: a whole 4x4x16 slice. The times are simulated.
512 devices in a mesh: stream: 16 (over z_lo, y), cross: 32 (over z_hi, x, core).
Axes of the slice: x: 4, y: 4, z: 16 (z_hi: 4, z_lo: 4; z = z_hi * 4 + z_lo), core: 2. Of those that a mesh axis runs over, the one named last changes fastest.
Arguments:
- vof: bfloat16 [6144, 512], P(('stream', 'cross')), may hold values from 0 to 1
- target: bfloat16 [6144, 512], P(('stream', 'cross')), may hold values from -21 to 21
- neighbours: int32 [6144, 26], P(('stream', 'cross')), may hold values from -1 to 6143, as said below
- live_blocks: int32 [512], P(('stream', 'cross')), may hold values from 2 to 12, as said below
- pick: int32 [512, 2], P(('stream', 'cross')), may hold values from -1 to 191, as said below
- w_first: bfloat16 [125, 128], replicated, may hold values from -0.5 to 0.5
- w_mid: bfloat16 [2, 128, 128], replicated, may hold values from -0.5 to 0.5
- w_last: bfloat16 [128], replicated, may hold values from -0.5 to 0.5
Outputs:
- prediction: float32 [4096, 512], P(('stream', 'cross'))
- grad_first: float32 [125, 128], replicated
- grad_mid: float32 [2, 128, 128], replicated
- grad_last: float32 [128], replicated
Inputs may be any that keep to these rules, and one draw needn't show every extreme that they name: Home slots 0 to live_blocks[d] - 1 of device d hold interface blocks and the rest are empty; in every slab 8 devices hold more than 6 blocks and the others at most 6. `neighbours`: an entry names a live home slot of a device whose stream index and cross index each differ from those of the block's own device by at most one. `pick`: in each slab every live home slot 6 + j of the device with cross index c is named, as c * 6 + j, by exactly one entry of one device of that slab; devices holding more than 6 blocks name none.
All inputs are finite; a program needn't handle non-finite values.
Results may differ from a plain program's by a relative error of at most 0.003.
The roundings to bfloat16 on the way count: a program that leaves them out, or rounds other values in their place, can miss the bound.
Values may be sent and summed in bfloat16 or wider, within the bound.
A program may use at most 128 MiB of HBM per device.

v0:
```python
import jax
import jax.numpy as jnp
from jax import lax
from jax.sharding import PartitionSpec as P

FEAT = 125
BE = 8
KEEP = 6
RECV = 2
PADROW = 1792


def from_behind(block, axis, distance):
    devices = range(lax.axis_size(axis))
    route = [(i - distance, i) for i in devices if i - distance in devices]
    return lax.ppermute(block, axis, route)


def assemble(center, border, block_edge):
    number = center.shape[0]
    pieces = jnp.concatenate([border[:, :13], center[:, None], border[:, 13:]], axis=1)
    shaped = pieces.reshape(number, 3, 3, 3, block_edge, block_edge, block_edge)
    shaped = shaped.transpose(0, 1, 4, 2, 5, 3, 6).reshape(
        number, 3 * block_edge, 3 * block_edge, 3 * block_edge
    )
    lower = block_edge - 2
    upper = 2 * block_edge + 2
    return shaped[:, lower:upper, lower:upper, lower:upper]


def stencil(padded, block_edge):
    columns = []
    for along_x in range(5):
        for along_y in range(5):
            for along_z in range(5):
                window = padded[
                    :,
                    along_x : along_x + block_edge,
                    along_y : along_y + block_edge,
                    along_z : along_z + block_edge,
                ]
                columns.append(window.reshape(-1))
    return jnp.stack(columns)


def contract_rows(former, latter):
    return lax.dot_general(
        former, latter, (((0,), (0,)), ((), ())), preferred_element_type=jnp.float32
    )


def contract_cols(former, latter):
    return lax.dot_general(
        former, latter, (((1,), (1,)), ((), ())), preferred_element_type=jnp.float32
    )


def train_terms(features, target_row, weight_mask, w_first, w_mid, w_last, loss_scale):
    hidden_one = jnp.tanh(contract_rows(w_first, features)).astype(jnp.bfloat16)
    hidden_two = jnp.tanh(contract_rows(w_mid[0], hidden_one)).astype(jnp.bfloat16)
    hidden_three = jnp.tanh(contract_rows(w_mid[1], hidden_two)).astype(jnp.bfloat16)
    predicted = jnp.dot(w_last, hidden_three, preferred_element_type=jnp.float32) * weight_mask
    residual = ((predicted - target_row.astype(jnp.float32)) * weight_mask / loss_scale).astype(
        jnp.bfloat16
    )
    grad_last = jnp.dot(hidden_three, residual, preferred_element_type=jnp.float32)
    slope_three = 1.0 - jnp.square(hidden_three.astype(jnp.float32))
    delta_three = (
        w_last.astype(jnp.float32)[:, None] * residual.astype(jnp.float32)[None, :] * slope_three
    ).astype(jnp.bfloat16)
    grad_third = contract_cols(hidden_two, delta_three)
    slope_two = 1.0 - jnp.square(hidden_two.astype(jnp.float32))
    delta_two = (
        jnp.dot(w_mid[1], delta_three, preferred_element_type=jnp.float32) * slope_two
    ).astype(jnp.bfloat16)
    grad_second = contract_cols(hidden_one, delta_two)
    slope_one = 1.0 - jnp.square(hidden_one.astype(jnp.float32))
    delta_one = (
        jnp.dot(w_mid[0], delta_two, preferred_element_type=jnp.float32) * slope_one
    ).astype(jnp.bfloat16)
    grad_first = contract_cols(features, delta_one)
    return (predicted, grad_first, jnp.stack([grad_second, grad_third]), grad_last)


def shards(vof, target, neighbours, live_blocks, pick, w_first, w_mid, w_last):
    home_blocks = vof.shape[0]
    cell_count = vof.shape[1]
    cross_size = lax.axis_size("cross")
    stream_size = lax.axis_size("stream")
    slab_index = lax.axis_index("stream")
    cross_index = lax.axis_index("cross")
    below = from_behind(vof, "stream", 1)
    above = from_behind(vof, "stream", -1)
    column = jnp.stack([below, vof, above])
    left = from_behind(column, "cross", 1)
    right = from_behind(column, "cross", -1)
    beside_all = jnp.stack([left, column, right], axis=1)
    table = jnp.concatenate(
        [beside_all.reshape(9 * home_blocks, cell_count), jnp.zeros((1, cell_count), vof.dtype)],
        axis=0,
    )
    owner_device = neighbours // home_blocks
    slab_step = owner_device // cross_size - slab_index + 1
    cross_step = owner_device % cross_size - cross_index + 1
    lookup = (slab_step * 3 + cross_step) * home_blocks + neighbours % home_blocks
    lookup = jnp.where(neighbours < 0, 9 * home_blocks, lookup)
    border = jnp.take(table, lookup, axis=0)
    padded = assemble(vof, border, BE)
    live_count = live_blocks[0]
    home_mask = (jnp.arange(home_blocks) < live_count).astype(jnp.float32)
    loss_scale = float(cell_count * KEEP * cross_size * stream_size)
    chosen = pick[0]
    padded_edge = padded.shape[1]
    flat_rows = padded.reshape(home_blocks, padded_edge**3)
    flat_rows = jnp.pad(flat_rows, ((0, 0), (0, PADROW - padded_edge**3)))
    pieces = (
        lax.all_gather(flat_rows[KEEP:], "cross", axis=0, tiled=True),
        lax.all_gather(target[KEEP:], "cross", axis=0, tiled=True),
    )
    selector = (chosen[:, None] == jnp.arange(pieces[0].shape[0])[None, :]).astype(jnp.bfloat16)
    got_blocks = jnp.dot(selector, pieces[0], preferred_element_type=jnp.float32)
    got_targets = jnp.dot(selector, pieces[1], preferred_element_type=jnp.float32)
    got_blocks = got_blocks.astype(jnp.bfloat16)
    got_targets = got_targets.astype(jnp.bfloat16)
    got_blocks = got_blocks[:, : padded_edge**3].reshape(
        RECV, padded_edge, padded_edge, padded_edge
    )
    work_padded = jnp.concatenate([padded[:KEEP], got_blocks], axis=0)
    work_target = jnp.concatenate([target[:KEEP], got_targets], axis=0)
    block_mask = jnp.concatenate([home_mask[:KEEP], (chosen >= 0).astype(jnp.float32)])
    predicted, grad_first, grad_mid, grad_last = train_terms(
        stencil(work_padded, BE),
        work_target.reshape(-1),
        jnp.repeat(block_mask, cell_count),
        w_first,
        w_mid,
        w_last,
        loss_scale,
    )
    prediction = predicted.reshape(KEEP + RECV, cell_count)
    hidden_size = grad_last.shape[0]
    packed = jnp.concatenate(
        [
            grad_first,
            grad_last[None, :],
            jnp.zeros((128 - FEAT - 1, hidden_size), jnp.float32),
            grad_mid.reshape(2 * hidden_size, hidden_size),
        ],
        axis=0,
    )
    summed = lax.psum(packed, ("stream", "cross"))
    return (
        prediction,
        summed[:FEAT],
        summed[128:].reshape(2, hidden_size, hidden_size),
        summed[FEAT],
    )


def solution(mesh):
    return jax.shard_map(
        shards,
        mesh=mesh,
        in_specs=(
            P(("stream", "cross"), None),
            P(("stream", "cross"), None),
            P(("stream", "cross"), None),
            P(("stream", "cross")),
            P(("stream", "cross"), None),
            P(),
            P(),
            P(),
        ),
        out_specs=(P(("stream", "cross"), None), P(), P(), P()),
        check_vma=False,
    )
```

profile of v0, /device:TPU:1, one launch (start us, length us, event | category | flops | bytes accessed | tf_op | source)
XLA Modules:
  0.0 796.8 jit_solution(742776914680141394)
XLA Ops:
  7.2 4.0 collective-permute-start
  11.3 1.3 collective-permute-start.1
  12.6 0.8 fusion.44
  13.4 60.5 %all-gather.1 = bf16[32,6,512]{2,1,0:T(8,128)(2,1)S(1)} all-gather(bf16[1,6,512]{2,1,0:T(8,128)(2,1)S(1)} %get-tuple-element.139), channel_id=1, replica_groups=mesh['stream'=16,'cross'=32] {'cross'}, dimensions={0}, use_global_device_ids=true | all-gather | bytes 202752 | tf_op jit(solution)/shard_map/all_gather | solution.py:118
  75.4 0.8 convolution_convert_fusion
  77.8 1.9 collective-permute-start.2
  79.7 2.4 collective-permute-start.3
  84.1 1.2 convert_element_type.65
  86.1 2.0 gather_fusion
  88.6 7.5 reshape.47
  96.0 12.7 %copy.151 = bf16[12,3,8,3,8,3,8]{0,6,5,4,3,2,1:T(8,128)(2,1)} copy(bf16[12,3,8,3,8,3,8]{6,4,2,5,3,1,0:T(8,128)(2,1)} %bitcast.318) | data formatting | bytes 663552 | tf_op jit(solution)/shard_map/transpose | solution.py:23
  108.7 1.4 slice.565
  110.2 1.4 slice.564
  112.1 53.0 %all-gather = bf16[32,6,1792]{2,1,0:T(8,128)(2,1)S(1)} all-gather(bf16[1,6,1792]{2,1,0:T(8,128)(2,1)S(1)} %fusion.18), channel_id=1, replica_groups=mesh['stream'=16,'cross'=32] {'cross'}, dimensions={0}, use_global_device_ids=true | all-gather | bytes 709632 | tf_op jit(solution)/shard_map/all_gather | solution.py:117
  165.8 1.0 copy.153
  167.3 1.2 slice_maximum_fusion.12
  168.4 1.2 slice_maximum_fusion.13
  169.6 1.2 slice_maximum_fusion.14
  170.8 1.3 slice_maximum_fusion.15
  172.1 1.2 slice_maximum_fusion.16
  173.4 1.1 slice_maximum_fusion.17
  174.5 1.2 slice_maximum_fusion.18
  175.7 1.3 slice_maximum_fusion.19
  176.9 1.3 slice_maximum_fusion.20
  178.2 1.3 slice_maximum_fusion.21
  179.4 1.3 slice_maximum_fusion.22
  180.7 1.1 slice_maximum_fusion.23
  181.8 1.3 slice_maximum_fusion.24
  183.1 1.3 slice_maximum_fusion.25
  184.4 1.3 slice_maximum_fusion.26
  185.6 1.3 slice_maximum_fusion.27
  186.9 1.2 slice_maximum_fusion.28
  188.0 1.2 slice_maximum_fusion.29
  189.2 1.2 slice_maximum_fusion.11
  190.4 1.3 slice_maximum_fusion.10
  191.6 1.2 slice_maximum_fusion.9
  192.9 1.1 slice_maximum_fusion.8
  194.0 1.4 slice_maximum_fusion.7
  195.4 1.2 slice_maximum_fusion.6
  196.6 1.3 slice_maximum_fusion.5
  197.9 1.2 slice_maximum_fusion.4
  199.1 1.1 slice_maximum_fusion.3
  209.2 1.2 copy.200
  212.5 0.8 stack_reshape.423
  216.8 0.8 stack_reshape.427
  235.2 0.8 stack_reshape.444
  241.6 0.8 stack_reshape.450
  252.2 0.8 stack_reshape.460
  253.3 0.8 stack_reshape.461
  266.5 0.8 stack_reshape.473
  269.7 0.8 stack_reshape.476
  277.2 0.8 stack_reshape.483
  281.1 1.2 copy.191
  293.2 0.8 stack_reshape.491
  310.7 9.6 %stack.44 = bf16[125,4096]{1,0:T(8,128)(2,1)S(1)} concatenate(bf16[1,4096]{1,0:T(2,128)(2,1)S(1)} %stack_reshape.375, bf16[1,4096]{1,0:T(2,128)(2,1)S(1)} %stack_reshape.376, bf16[1,4096]{1,0:T(2,128)(2,1)S(1)} %stack_reshape.377, bf16[1,4096]{1,0:T(2,128)(2,1)S(1)} %stack_reshape.378, bf16[1,4096]{1,0:T(2,128)(2,1)S(1)} %stack_reshape.379, bf16[1,4096]{1,0:T(2,128)(2,1)S(1)} %stack_reshape.380, ...), dimensions={0} | concatenate | bytes 2048000 | tf_op jit(solution)/shard_map/stack | solution.py:43
  322.2 1.8 fusion.3
  324.0 2.1 fusion.6
  326.1 1.8 convolution_bitcast_fusion.1
  327.9 1.1 convolution_bitcast_fusion
  329.3 0.8 pad_maximum_fusion.1
  330.7 454.9 %all-reduce.4.cloned.1.call-done = f32[384,128]{1,0:T(8,128)} async-done(((f32[384,128]{1,0:T(8,128)}), f32[384,128]{1,0:T(8,128)}) %all-reduce.4.cloned.1.call-update) | async-done | bytes 196624 | tf_op jit(solution)/shard_map/psum | solution.py:151
  785.5 1.6 slice.816
  787.1 1.5 slice.815
  788.6 1.2 slice_bitcast_fusion.1
  (594 shorter events, 107.9 us)
Async XLA Ops:
  7.2 313.1 %copy-start = (bf16[125,128]{1,0:T(8,128)(2,1)S(1)}, bf16[125,128]{1,0:T(8,128)(2,1)}, u32[]{:S(2)}) copy-start(bf16[125,128]{1,0:T(8,128)(2,1)} %param.13) | copy-start | bytes 96004
  7.2 778.4 %all-reduce.4.cloned.1.call-start = ((), (), s32[]{:S(2)}) async-start(), calls=%async_computation | async-start | bytes 393216 | tf_op jit(solution)/shard_map/psum | solution.py:151
  7.2 69.8 %collective-permute-start = (bf16[12,512]{1,0:T(8,128)(2,1)}, bf16[12,512]{1,0:T(8,128)(2,1)S(1)}, u32[]{:S(2)}, u32[]{:S(2)}) collective-permute-start(bf16[12,512]{1,0:T(8,128)(2,1)} %param.8), channel_id=1, source_target_pairs={{0,32},{32,64},{64,96},{96,128},{128,160},{160,192},{192,224},{224... | collective-permute-start | bytes 36872 | tf_op jit(solution)/shard_map/ppermute | solution.py:16
  11.3 65.8 %collective-permute-start.1 = (bf16[12,512]{1,0:T(8,128)(2,1)}, bf16[12,512]{1,0:T(8,128)(2,1)S(1)}, u32[]{:S(2)}, u32[]{:S(2)}) collective-permute-start(bf16[12,512]{1,0:T(8,128)(2,1)} %param.8), channel_id=1, source_target_pairs={{32,0},{64,32},{96,64},{128,96},{160,128},{192,160},{224,192},{256... | collective-permute-start | bytes 36872 | tf_op jit(solution)/shard_map/ppermute | solution.py:16
  77.8 8.2 %collective-permute-start.2 = (bf16[3,12,512]{2,1,0:T(8,128)(2,1)S(1)}, bf16[3,12,512]{2,1,0:T(8,128)(2,1)S(1)}, u32[]{:S(2)}, u32[]{:S(2)}) collective-permute-start(bf16[3,12,512]{2,1,0:T(8,128)(2,1)S(1)} %get-tuple-element.137), channel_id=1, source_target_pairs={{0,1},{1,2},{2,3},{3,4},{4,5},{5,6},{6,7},{7,8},{8,9},{9,10},{10,1... | collective-permute-start | bytes 110600 | tf_op jit(solution)/shard_map/ppermute | solution.py:16
  79.7 6.2 collective-permute-start.3
  111.6 53.7 %copy-start.151 = (s32[1,2]{1,0:T(1,128)S(1)}, s32[1,2]{1,0:T(1,128)}, u32[]{:S(2)}) copy-start(s32[1,2]{1,0:T(1,128)} %param.12) | copy-start | bytes 28
  204.8 11.7 %copy-start.97 = (bf16[8,8,8,8]{0,3,2,1:T(8,128)(2,1)S(1)}, bf16[8,8,8,8]{0,3,2,1:T(8,128)(2,1)}, u32[]{:S(2)}) copy-start(bf16[8,8,8,8]{0,3,2,1:T(8,128)(2,1)} %get-tuple-element.79) | copy-start | bytes 24580
  205.2 12.3 %copy-start.96 = (bf16[8,8,8,8]{0,3,2,1:T(8,128)(2,1)S(1)}, bf16[8,8,8,8]{0,3,2,1:T(8,128)(2,1)}, u32[]{:S(2)}) copy-start(bf16[8,8,8,8]{0,3,2,1:T(8,128)(2,1)} %get-tuple-element.80) | copy-start | bytes 24580
  206.3 12.3 %copy-start.95 = (bf16[8,8,8,8]{0,3,2,1:T(8,128)(2,1)S(1)}, bf16[8,8,8,8]{0,3,2,1:T(8,128)(2,1)}, u32[]{:S(2)}) copy-start(bf16[8,8,8,8]{0,3,2,1:T(8,128)(2,1)} %get-tuple-element.81) | copy-start | bytes 24580
  207.4 12.3 %copy-start.94 = (bf16[8,8,8,8]{0,3,2,1:T(8,128)(2,1)S(1)}, bf16[8,8,8,8]{0,3,2,1:T(8,128)(2,1)}, u32[]{:S(2)}) copy-start(bf16[8,8,8,8]{0,3,2,1:T(8,128)(2,1)} %get-tuple-element.83) | copy-start | bytes 24580
  208.4 12.3 %copy-start.93 = (bf16[8,8,8,8]{0,3,2,1:T(8,128)(2,1)S(1)}, bf16[8,8,8,8]{0,3,2,1:T(8,128)(2,1)}, u32[]{:S(2)}) copy-start(bf16[8,8,8,8]{0,3,2,1:T(8,128)(2,1)} %get-tuple-element.84) | copy-start | bytes 24580
  210.4 11.5 %copy-start.92 = (bf16[8,8,8,8]{0,3,2,1:T(8,128)(2,1)S(1)}, bf16[8,8,8,8]{0,3,2,1:T(8,128)(2,1)}, u32[]{:S(2)}) copy-start(bf16[8,8,8,8]{0,3,2,1:T(8,128)(2,1)} %get-tuple-element.85) | copy-start | bytes 24580
  211.5 11.5 %copy-start.91 = (bf16[8,8,8,8]{0,3,2,1:T(8,128)(2,1)S(1)}, bf16[8,8,8,8]{0,3,2,1:T(8,128)(2,1)}, u32[]{:S(2)}) copy-start(bf16[8,8,8,8]{0,3,2,1:T(8,128)(2,1)} %get-tuple-element.87) | copy-start | bytes 24580
  212.5 11.5 %copy-start.90 = (bf16[8,8,8,8]{0,3,2,1:T(8,128)(2,1)S(1)}, bf16[8,8,8,8]{0,3,2,1:T(8,128)(2,1)}, u32[]{:S(2)}) copy-start(bf16[8,8,8,8]{0,3,2,1:T(8,128)(2,1)} %get-tuple-element.88) | copy-start | bytes 24580
  213.6 11.7 %copy-start.89 = (bf16[8,8,8,8]{0,3,2,1:T(8,128)(2,1)S(1)}, bf16[8,8,8,8]{0,3,2,1:T(8,128)(2,1)}, u32[]{:S(2)}) copy-start(bf16[8,8,8,8]{0,3,2,1:T(8,128)(2,1)} %get-tuple-element.89) | copy-start | bytes 24580
  214.7 11.7 %copy-start.88 = (bf16[8,8,8,8]{0,3,2,1:T(8,128)(2,1)S(1)}, bf16[8,8,8,8]{0,3,2,1:T(8,128)(2,1)}, u32[]{:S(2)}) copy-start(bf16[8,8,8,8]{0,3,2,1:T(8,128)(2,1)} %get-tuple-element.91) | copy-start | bytes 24580
  215.7 11.7 %copy-start.87 = (bf16[8,8,8,8]{0,3,2,1:T(8,128)(2,1)S(1)}, bf16[8,8,8,8]{0,3,2,1:T(8,128)(2,1)}, u32[]{:S(2)}) copy-start(bf16[8,8,8,8]{0,3,2,1:T(8,128)(2,1)} %get-tuple-element.92) | copy-start | bytes 24580
  216.8 11.7 %copy-start.86 = (bf16[8,8,8,8]{0,3,2,1:T(8,128)(2,1)S(1)}, bf16[8,8,8,8]{0,3,2,1:T(8,128)(2,1)}, u32[]{:S(2)}) copy-start(bf16[8,8,8,8]{0,3,2,1:T(8,128)(2,1)} %get-tuple-element.93) | copy-start | bytes 24580
  217.9 11.7 %copy-start.85 = (bf16[8,8,8,8]{0,3,2,1:T(8,128)(2,1)S(1)}, bf16[8,8,8,8]{0,3,2,1:T(8,128)(2,1)}, u32[]{:S(2)}) copy-start(bf16[8,8,8,8]{0,3,2,1:T(8,128)(2,1)} %get-tuple-element.95) | copy-start | bytes 24580
  218.9 11.6 %copy-start.84 = (bf16[8,8,8,8]{0,3,2,1:T(8,128)(2,1)S(1)}, bf16[8,8,8,8]{0,3,2,1:T(8,128)(2,1)}, u32[]{:S(2)}) copy-start(bf16[8,8,8,8]{0,3,2,1:T(8,128)(2,1)} %get-tuple-element.96) | copy-start | bytes 24580
  220.0 11.6 %copy-start.83 = (bf16[8,8,8,8]{0,3,2,1:T(8,128)(2,1)S(1)}, bf16[8,8,8,8]{0,3,2,1:T(8,128)(2,1)}, u32[]{:S(2)}) copy-start(bf16[8,8,8,8]{0,3,2,1:T(8,128)(2,1)} %get-tuple-element.97) | copy-start | bytes 24580
  221.1 11.6 %copy-start.82 = (bf16[8,8,8,8]{0,3,2,1:T(8,128)(2,1)S(1)}, bf16[8,8,8,8]{0,3,2,1:T(8,128)(2,1)}, u32[]{:S(2)}) copy-start(bf16[8,8,8,8]{0,3,2,1:T(8,128)(2,1)} %get-tuple-element.99) | copy-start | bytes 24580
  222.1 11.7 %copy-start.81 = (bf16[8,8,8,8]{0,3,2,1:T(8,128)(2,1)S(1)}, bf16[8,8,8,8]{0,3,2,1:T(8,128)(2,1)}, u32[]{:S(2)}) copy-start(bf16[8,8,8,8]{0,3,2,1:T(8,128)(2,1)} %get-tuple-element.100) | copy-start | bytes 24580
  223.2 11.6 %copy-start.80 = (bf16[8,8,8,8]{0,3,2,1:T(8,128)(2,1)S(1)}, bf16[8,8,8,8]{0,3,2,1:T(8,128)(2,1)}, u32[]{:S(2)}) copy-start(bf16[8,8,8,8]{0,3,2,1:T(8,128)(2,1)} %get-tuple-element.101) | copy-start | bytes 24580
  224.5 11.4 %copy-start.79 = (bf16[8,8,8,8]{0,3,2,1:T(8,128)(2,1)S(1)}, bf16[8,8,8,8]{0,3,2,1:T(8,128)(2,1)}, u32[]{:S(2)}) copy-start(bf16[8,8,8,8]{0,3,2,1:T(8,128)(2,1)} %get-tuple-element.103) | copy-start | bytes 24580
  225.6 11.5 %copy-start.78 = (bf16[8,8,8,8]{0,3,2,1:T(8,128)(2,1)S(1)}, bf16[8,8,8,8]{0,3,2,1:T(8,128)(2,1)}, u32[]{:S(2)}) copy-start(bf16[8,8,8,8]{0,3,2,1:T(8,128)(2,1)} %get-tuple-element.104) | copy-start | bytes 24580
  226.6 11.4 %copy-start.77 = (bf16[8,8,8,8]{0,3,2,1:T(8,128)(2,1)S(1)}, bf16[8,8,8,8]{0,3,2,1:T(8,128)(2,1)}, u32[]{:S(2)}) copy-start(bf16[8,8,8,8]{0,3,2,1:T(8,128)(2,1)} %get-tuple-element.105) | copy-start | bytes 24580
  227.7 11.5 %copy-start.76 = (bf16[8,8,8,8]{0,3,2,1:T(8,128)(2,1)S(1)}, bf16[8,8,8,8]{0,3,2,1:T(8,128)(2,1)}, u32[]{:S(2)}) copy-start(bf16[8,8,8,8]{0,3,2,1:T(8,128)(2,1)} %get-tuple-element.107) | copy-start | bytes 24580
  228.8 11.5 %copy-start.75 = (bf16[8,8,8,8]{0,3,2,1:T(8,128)(2,1)S(1)}, bf16[8,8,8,8]{0,3,2,1:T(8,128)(2,1)}, u32[]{:S(2)}) copy-start(bf16[8,8,8,8]{0,3,2,1:T(8,128)(2,1)} %get-tuple-element.108) | copy-start | bytes 24580
  229.8 11.5 %copy-start.74 = (bf16[8,8,8,8]{0,3,2,1:T(8,128)(2,1)S(1)}, bf16[8,8,8,8]{0,3,2,1:T(8,128)(2,1)}, u32[]{:S(2)}) copy-start(bf16[8,8,8,8]{0,3,2,1:T(8,128)(2,1)} %get-tuple-element.109) | copy-start | bytes 24580
  230.9 11.5 %copy-start.73 = (bf16[8,8,8,8]{0,3,2,1:T(8,128)(2,1)S(1)}, bf16[8,8,8,8]{0,3,2,1:T(8,128)(2,1)}, u32[]{:S(2)}) copy-start(bf16[8,8,8,8]{0,3,2,1:T(8,128)(2,1)} %get-tuple-element.111) | copy-start | bytes 24580
  232.0 11.5 %copy-start.72 = (bf16[8,8,8,8]{0,3,2,1:T(8,128)(2,1)S(1)}, bf16[8,8,8,8]{0,3,2,1:T(8,128)(2,1)}, u32[]{:S(2)}) copy-start(bf16[8,8,8,8]{0,3,2,1:T(8,128)(2,1)} %get-tuple-element.112) | copy-start | bytes 24580
  233.0 11.4 %copy-start.71 = (bf16[8,8,8,8]{0,3,2,1:T(8,128)(2,1)S(1)}, bf16[8,8,8,8]{0,3,2,1:T(8,128)(2,1)}, u32[]{:S(2)}) copy-start(bf16[8,8,8,8]{0,3,2,1:T(8,128)(2,1)} %get-tuple-element.113) | copy-start | bytes 24580
  234.1 11.4 %copy-start.70 = (bf16[8,8,8,8]{0,3,2,1:T(8,128)(2,1)S(1)}, bf16[8,8,8,8]{0,3,2,1:T(8,128)(2,1)}, u32[]{:S(2)}) copy-start(bf16[8,8,8,8]{0,3,2,1:T(8,128)(2,1)} %get-tuple-element.115) | copy-start | bytes 24580
  235.2 11.4 %copy-start.69 = (bf16[8,8,8,8]{0,3,2,1:T(8,128)(2,1)S(1)}, bf16[8,8,8,8]{0,3,2,1:T(8,128)(2,1)}, u32[]{:S(2)}) copy-start(bf16[8,8,8,8]{0,3,2,1:T(8,128)(2,1)} %get-tuple-element.116) | copy-start | bytes 24580
  241.6 11.4 %copy-start.63 = (bf16[8,8,8,8]{0,3,2,1:T(8,128)(2,1)S(1)}, bf16[8,8,8,8]{0,3,2,1:T(8,128)(2,1)}, u32[]{:S(2)}) copy-start(bf16[8,8,8,8]{0,3,2,1:T(8,128)(2,1)} %get-tuple-element.124) | copy-start | bytes 24580
  242.6 11.4 %copy-start.62 = (bf16[8,8,8,8]{0,3,2,1:T(8,128)(2,1)S(1)}, bf16[8,8,8,8]{0,3,2,1:T(8,128)(2,1)}, u32[]{:S(2)}) copy-start(bf16[8,8,8,8]{0,3,2,1:T(8,128)(2,1)} %get-tuple-element.125) | copy-start | bytes 24580
  243.7 11.5 %copy-start.61 = (bf16[8,8,8,8]{0,3,2,1:T(8,128)(2,1)S(1)}, bf16[8,8,8,8]{0,3,2,1:T(8,128)(2,1)}, u32[]{:S(2)}) copy-start(bf16[8,8,8,8]{0,3,2,1:T(8,128)(2,1)} %get-tuple-element.127) | copy-start | bytes 24580
  244.8 11.5 %copy-start.60 = (bf16[8,8,8,8]{0,3,2,1:T(8,128)(2,1)S(1)}, bf16[8,8,8,8]{0,3,2,1:T(8,128)(2,1)}, u32[]{:S(2)}) copy-start(bf16[8,8,8,8]{0,3,2,1:T(8,128)(2,1)} %get-tuple-element.128) | copy-start | bytes 24580
  245.8 11.5 %copy-start.59 = (bf16[8,8,8,8]{0,3,2,1:T(8,128)(2,1)S(1)}, bf16[8,8,8,8]{0,3,2,1:T(8,128)(2,1)}, u32[]{:S(2)}) copy-start(bf16[8,8,8,8]{0,3,2,1:T(8,128)(2,1)} %get-tuple-element.129) | copy-start | bytes 24580
  246.9 11.5 %copy-start.58 = (bf16[8,8,8,8]{0,3,2,1:T(8,128)(2,1)S(1)}, bf16[8,8,8,8]{0,3,2,1:T(8,128)(2,1)}, u32[]{:S(2)}) copy-start(bf16[8,8,8,8]{0,3,2,1:T(8,128)(2,1)} %get-tuple-element.131) | copy-start | bytes 24580
  248.0 11.5 %copy-start.57 = (bf16[8,8,8,8]{0,3,2,1:T(8,128)(2,1)S(1)}, bf16[8,8,8,8]{0,3,2,1:T(8,128)(2,1)}, u32[]{:S(2)}) copy-start(bf16[8,8,8,8]{0,3,2,1:T(8,128)(2,1)} %get-tuple-element.132) | copy-start | bytes 24580
  249.0 11.4 %copy-start.56 = (bf16[8,8,8,8]{0,3,2,1:T(8,128)(2,1)S(1)}, bf16[8,8,8,8]{0,3,2,1:T(8,128)(2,1)}, u32[]{:S(2)}) copy-start(bf16[8,8,8,8]{0,3,2,1:T(8,128)(2,1)} %get-tuple-element.133) | copy-start | bytes 24580
  250.1 11.8 %copy-start.55 = (bf16[8,8,8,8]{0,3,2,1:T(8,128)(2,1)S(1)}, bf16[8,8,8,8]{0,3,2,1:T(8,128)(2,1)}, u32[]{:S(2)}) copy-start(bf16[8,8,8,8]{0,3,2,1:T(8,128)(2,1)} %get-tuple-element.130) | copy-start | bytes 24580
  251.2 11.8 %copy-start.54 = (bf16[8,8,8,8]{0,3,2,1:T(8,128)(2,1)S(1)}, bf16[8,8,8,8]{0,3,2,1:T(8,128)(2,1)}, u32[]{:S(2)}) copy-start(bf16[8,8,8,8]{0,3,2,1:T(8,128)(2,1)} %get-tuple-element.126) | copy-start | bytes 24580
  252.2 11.8 %copy-start.53 = (bf16[8,8,8,8]{0,3,2,1:T(8,128)(2,1)S(1)}, bf16[8,8,8,8]{0,3,2,1:T(8,128)(2,1)}, u32[]{:S(2)}) copy-start(bf16[8,8,8,8]{0,3,2,1:T(8,128)(2,1)} %get-tuple-element.122) | copy-start | bytes 24580
  253.3 11.8 %copy-start.52 = (bf16[8,8,8,8]{0,3,2,1:T(8,128)(2,1)S(1)}, bf16[8,8,8,8]{0,3,2,1:T(8,128)(2,1)}, u32[]{:S(2)}) copy-start(bf16[8,8,8,8]{0,3,2,1:T(8,128)(2,1)} %get-tuple-element.118) | copy-start | bytes 24580
  254.4 11.8 %copy-start.51 = (bf16[8,8,8,8]{0,3,2,1:T(8,128)(2,1)S(1)}, bf16[8,8,8,8]{0,3,2,1:T(8,128)(2,1)}, u32[]{:S(2)}) copy-start(bf16[8,8,8,8]{0,3,2,1:T(8,128)(2,1)} %get-tuple-element.114) | copy-start | bytes 24580
  255.4 11.8 %copy-start.50 = (bf16[8,8,8,8]{0,3,2,1:T(8,128)(2,1)S(1)}, bf16[8,8,8,8]{0,3,2,1:T(8,128)(2,1)}, u32[]{:S(2)}) copy-start(bf16[8,8,8,8]{0,3,2,1:T(8,128)(2,1)} %get-tuple-element.110) | copy-start | bytes 24580
  256.5 11.8 %copy-start.49 = (bf16[8,8,8,8]{0,3,2,1:T(8,128)(2,1)S(1)}, bf16[8,8,8,8]{0,3,2,1:T(8,128)(2,1)}, u32[]{:S(2)}) copy-start(bf16[8,8,8,8]{0,3,2,1:T(8,128)(2,1)} %get-tuple-element.106) | copy-start | bytes 24580
  257.6 11.8 %copy-start.48 = (bf16[8,8,8,8]{0,3,2,1:T(8,128)(2,1)S(1)}, bf16[8,8,8,8]{0,3,2,1:T(8,128)(2,1)}, u32[]{:S(2)}) copy-start(bf16[8,8,8,8]{0,3,2,1:T(8,128)(2,1)} %get-tuple-element.102) | copy-start | bytes 24580
  258.6 11.8 %copy-start.47 = (bf16[8,8,8,8]{0,3,2,1:T(8,128)(2,1)S(1)}, bf16[8,8,8,8]{0,3,2,1:T(8,128)(2,1)}, u32[]{:S(2)}) copy-start(bf16[8,8,8,8]{0,3,2,1:T(8,128)(2,1)} %get-tuple-element.98) | copy-start | bytes 24580
  259.7 11.8 %copy-start.46 = (bf16[8,8,8,8]{0,3,2,1:T(8,128)(2,1)S(1)}, bf16[8,8,8,8]{0,3,2,1:T(8,128)(2,1)}, u32[]{:S(2)}) copy-start(bf16[8,8,8,8]{0,3,2,1:T(8,128)(2,1)} %get-tuple-element.94) | copy-start | bytes 24580
  261.1 11.5 %copy-start.41 = (bf16[8,8,8,8]{0,3,2,1:T(8,128)(2,1)S(1)}, bf16[8,8,8,8]{0,3,2,1:T(8,128)(2,1)}, u32[]{:S(2)}) copy-start(bf16[8,8,8,8]{0,3,2,1:T(8,128)(2,1)} %get-tuple-element.90) | copy-start | bytes 24580
  262.2 11.5 %copy-start.37 = (bf16[8,8,8,8]{0,3,2,1:T(8,128)(2,1)S(1)}, bf16[8,8,8,8]{0,3,2,1:T(8,128)(2,1)}, u32[]{:S(2)}) copy-start(bf16[8,8,8,8]{0,3,2,1:T(8,128)(2,1)} %get-tuple-element.86) | copy-start | bytes 24580
  263.3 11.5 %copy-start.33 = (bf16[8,8,8,8]{0,3,2,1:T(8,128)(2,1)S(1)}, bf16[8,8,8,8]{0,3,2,1:T(8,128)(2,1)}, u32[]{:S(2)}) copy-start(bf16[8,8,8,8]{0,3,2,1:T(8,128)(2,1)} %get-tuple-element.82) | copy-start | bytes 24580
  264.3 11.5 %copy-start.28 = (bf16[8,8,8,8]{0,3,2,1:T(8,128)(2,1)S(1)}, bf16[8,8,8,8]{0,3,2,1:T(8,128)(2,1)}, u32[]{:S(2)}) copy-start(bf16[8,8,8,8]{0,3,2,1:T(8,128)(2,1)} %get-tuple-element.78) | copy-start | bytes 24580
  265.4 11.4 %copy-start.24 = (bf16[8,8,8,8]{0,3,2,1:T(8,128)(2,1)S(1)}, bf16[8,8,8,8]{0,3,2,1:T(8,128)(2,1)}, u32[]{:S(2)}) copy-start(bf16[8,8,8,8]{0,3,2,1:T(8,128)(2,1)} %get-tuple-element.74) | copy-start | bytes 24580
  266.5 11.5 %copy-start.20 = (bf16[8,8,8,8]{0,3,2,1:T(8,128)(2,1)S(1)}, bf16[8,8,8,8]{0,3,2,1:T(8,128)(2,1)}, u32[]{:S(2)}) copy-start(bf16[8,8,8,8]{0,3,2,1:T(8,128)(2,1)} %get-tuple-element.70) | copy-start | bytes 24580
  267.6 11.5 %copy-start.15 = (bf16[8,8,8,8]{0,3,2,1:T(8,128)(2,1)S(1)}, bf16[8,8,8,8]{0,3,2,1:T(8,128)(2,1)}, u32[]{:S(2)}) copy-start(bf16[8,8,8,8]{0,3,2,1:T(8,128)(2,1)} %get-tuple-element.66) | copy-start | bytes 24580
  268.6 11.5 %copy-start.11 = (bf16[8,8,8,8]{0,3,2,1:T(8,128)(2,1)S(1)}, bf16[8,8,8,8]{0,3,2,1:T(8,128)(2,1)}, u32[]{:S(2)}) copy-start(bf16[8,8,8,8]{0,3,2,1:T(8,128)(2,1)} %get-tuple-element.62) | copy-start | bytes 24580
  270.8 12.4 %copy-start.45 = (bf16[8,8,8,8]{0,3,2,1:T(8,128)(2,1)S(1)}, bf16[8,8,8,8]{0,3,2,1:T(8,128)(2,1)}, u32[]{:S(2)}) copy-start(bf16[8,8,8,8]{0,3,2,1:T(8,128)(2,1)} %get-tuple-element.60) | copy-start | bytes 24580
  271.8 11.8 %copy-start.44 = (bf16[8,8,8,8]{0,3,2,1:T(8,128)(2,1)S(1)}, bf16[8,8,8,8]{0,3,2,1:T(8,128)(2,1)}, u32[]{:S(2)}) copy-start(bf16[8,8,8,8]{0,3,2,1:T(8,128)(2,1)} %get-tuple-element.61) | copy-start | bytes 24580
  (95 other events, 592.5 us)
Sparse Core Ops, SparseCore 0:
  330.2 455.2 all-reduce.3
where the time goes:
time: 803 us; the launch traced here: 797 us
  waiting for transfers between devices  455 us (57%)
  local copies, waits for them, and re-layouts  152 us (19%)
  blocking collectives  114 us (14%)
  other arithmetic  39.4 us (5%)
  between operations  17.8 us (2%)
  matrix products  9.76 us (1%)
  starting transfers between devices  9.69 us (1%)
    psum x1, waiting for transfers between devices, shards(): summed = lax.psum(packed, ('stream', 'cross'))  455 us
    another operation x126, local copies, waits for them, and re-layouts, stencil(): return jnp.stack(columns)  77.5 us
    all_gather x1, blocking collectives, shards(): lax.all_gather(target[KEEP:], 'cross', axis=0, tiled=True)  60.5 us
    all_gather x1, blocking collectives, shards(): lax.all_gather(flat_rows[KEEP:], 'cross', axis=0, tiled=True)  53 us
    slice x125, local copies, waits for them, and re-layouts, stencil(): padded[:, along_x:along_x + block_edge, along_y:along_y + block_edge, alo...  38.1 us
    concatenate x31, other arithmetic, shards(): work_padded = jnp.concatenate([padded[:KEEP], got_blocks], axis=0)  34.8 us
  transfers between devices with their start and end apart: 5, of which 1 were waited for; matrix products, arithmetic and copies ran while one was open for 1% of the time, Pallas kernels for 0%

commit v1 on v0

--- a/solution.py
+++ b/solution.py
@@ -115,7 +115,15 @@
     flat_rows = jnp.pad(flat_rows, ((0, 0), (0, PADROW - padded_edge**3)))
     pieces = (
         lax.all_gather(flat_rows[KEEP:], "cross", axis=0, tiled=True),
-        lax.all_gather(target[KEEP:], "cross", axis=0, tiled=True),
+        jnp.concatenate(
+            lax.all_to_all(
+                jnp.stack([target[KEEP:]] * lax.axis_size("cross"), axis=0),
+                axis_name="cross",
+                split_axis=0,
+                concat_axis=0,
+            ),
+            0,
+        ),
     )
     selector = (chosen[:, None] == jnp.arange(pieces[0].shape[0])[None, :]).astype(jnp.bfloat16)
     got_blocks = jnp.dot(selector, pieces[0], preferred_element_type=jnp.float32)

time: 803 us -> 779 us (0.970)
  blocking collectives: 114 us -> 57.4 us
  starting transfers between devices: 9.69 us -> 29.5 us
    all_gather x1 -> x0, blocking collectives: 60.5 us -> none  [shards(): lax.all_gather(target[KEEP:], 'cross', axis=0, tiled=True)]
    all_to_all x0 -> x1, starting transfers between devices: none -> 18.7 us  [shards(): lax.all_to_all(jnp.stack([target[KEEP:]] * lax.axis_size('cross'), axis=0...]
  transfers between devices with their start and end apart: 5 -> 6, of which waited for: 1 -> 2; matrix products, arithmetic and copies ran while one was open for 1% -> 25% of each run, Pallas kernels for 0% -> 0%
where the time goes in v1:
time: 779 us; the launch traced here: 773 us
  waiting for transfers between devices  456 us (59%)
  local copies, waits for them, and re-layouts  160 us (21%)
  blocking collectives  57.4 us (7%)
  other arithmetic  40.1 us (5%)
  starting transfers between devices  29.5 us (4%)
  between operations  17.9 us (2%)
  matrix products  11.7 us (2%)
    psum x1, waiting for transfers between devices, shards(): summed = lax.psum(packed, ('stream', 'cross'))  455 us
    another operation x126, local copies, waits for them, and re-layouts, stencil(): return jnp.stack(columns)  82.3 us
    all_gather x1, blocking collectives, shards(): lax.all_gather(flat_rows[KEEP:], 'cross', axis=0, tiled=True)  57.4 us
    slice x125, local copies, waits for them, and re-layouts, stencil(): padded[:, along_x:along_x + block_edge, along_y:along_y + block_edge, alo...  39.3 us
    concatenate x31, other arithmetic, shards(): work_padded = jnp.concatenate([padded[:KEEP], got_blocks], axis=0)  35.6 us
    all_to_all x1, starting transfers between devices, shards(): lax.all_to_all(jnp.stack([target[KEEP:]] * lax.axis_size('cross'), axis=0...  18.7 us
  transfers between devices with their start and end apart: 6, of which 2 were waited for; matrix products, arithmetic and copies ran while one was open for 25% of the time, Pallas kernels for 0%

profile of v1, /device:TPU:1, one launch (start us, length us, event | category | flops | bytes accessed | tf_op | source)
XLA Modules:
  0.0 772.6 jit_solution(3373470099756317012)
XLA Ops:
  7.2 4.0 collective-permute-start
  11.2 1.3 collective-permute-start.1
  12.5 1.4 fusion.44
  14.6 18.7 %all-to-all-start = ((bf16[32,6,512]{2,1,0:T(8,128)(2,1)}), bf16[32,6,512]{2,1,0:T(8,128)(2,1)S(1)}, u32[]{:S(2)}, u32[]{:S(2)}) async-start(bf16[32,6,512]{2,1,0:T(8,128)(2,1)} %stack.35), calls=%async_computation | async-start | bytes 524288 | tf_op jit(solution)/shard_map/all_to_all | solution.py:119
  36.4 3.5 collective-permute-start.2
  39.9 1.9 collective-permute-start.3
  43.2 1.2 convert_element_type.65
  45.8 2.0 gather_fusion
  48.2 7.5 reshape.52
  55.7 12.7 %copy.151 = bf16[12,3,8,3,8,3,8]{0,6,5,4,3,2,1:T(8,128)(2,1)} copy(bf16[12,3,8,3,8,3,8]{6,4,2,5,3,1,0:T(8,128)(2,1)} %bitcast.316) | data formatting | bytes 663552 | tf_op jit(solution)/shard_map/transpose | solution.py:23
  68.4 1.4 slice.565
  69.8 1.4 slice.564
  71.7 57.4 %all-gather = bf16[32,6,1792]{2,1,0:T(8,128)(2,1)S(1)} all-gather(bf16[1,6,1792]{2,1,0:T(8,128)(2,1)S(1)} %fusion.18), channel_id=1, replica_groups=mesh['stream'=16,'cross'=32] {'cross'}, dimensions={0}, use_global_device_ids=true | all-gather | bytes 709632 | tf_op jit(solution)/shard_map/all_gather | solution.py:117
  129.7 1.0 copy.153
  131.3 1.2 slice_maximum_fusion.12
  132.4 1.1 slice_maximum_fusion.13
  133.6 1.3 slice_maximum_fusion.14
  134.9 1.3 slice_maximum_fusion.15
  136.2 1.3 slice_maximum_fusion.16
  137.4 1.1 slice_maximum_fusion.17
  138.6 1.1 slice_maximum_fusion.18
  139.7 1.3 slice_maximum_fusion.19
  141.0 1.3 slice_maximum_fusion.20
  142.2 1.2 slice_maximum_fusion.21
  143.5 1.2 slice_maximum_fusion.22
  144.7 1.1 slice_maximum_fusion.23
  145.9 1.3 slice_maximum_fusion.24
  147.1 1.3 slice_maximum_fusion.25
  148.4 1.2 slice_maximum_fusion.26
  149.7 1.2 slice_maximum_fusion.27
  150.9 1.2 slice_maximum_fusion.28
  152.0 1.2 slice_maximum_fusion.29
  153.2 1.2 slice_maximum_fusion.11
  154.4 1.3 slice_maximum_fusion.10
  155.7 1.3 slice_maximum_fusion.9
  157.0 1.1 slice_maximum_fusion.8
  158.1 1.4 slice_maximum_fusion.7
  159.5 1.2 slice_maximum_fusion.6
  160.7 1.2 slice_maximum_fusion.5
  161.9 1.2 slice_maximum_fusion.4
  163.1 1.2 slice_maximum_fusion.3
  164.3 1.1 slice_maximum_fusion.2
  168.1 0.8 stack_reshape.378
  172.4 0.8 stack_reshape.417
  176.4 1.2 copy.200
  201.2 0.8 stack_reshape.443
  226.9 1.2 stack_reshape.467
  240.0 0.8 stack_reshape.479
  244.3 0.8 stack_reshape.483
  248.3 1.2 copy.191
  250.2 1.2 copy.192
  252.2 1.2 copy.193
  280.8 10.4 %stack.34 = bf16[125,4096]{1,0:T(8,128)(2,1)S(1)} concatenate(bf16[1,4096]{1,0:T(2,128)(2,1)S(1)} %stack_reshape.375, bf16[1,4096]{1,0:T(2,128)(2,1)S(1)} %stack_reshape.376, bf16[1,4096]{1,0:T(2,128)(2,1)S(1)} %stack_reshape.377, bf16[1,4096]{1,0:T(2,128)(2,1)S(1)} %copy-done.110, bf16[1,4096]{1,0:T(2,128)(2,1)S(1)} %stack_reshape.379, bf16[1,4096]{1,0:T(2,128)(2,1)S(1)} %stack_reshape.380, ...), dimensions={0} | concatenate | bytes 2048000 | tf_op jit(solution)/shard_map/stack | solution.py:43
  292.1 1.0 copy-done.1
  294.7 1.1 convolution_convert_fusion
  295.9 2.8 fusion.3
  298.7 2.7 fusion.6
  301.4 1.8 convolution_bitcast_fusion.1
  303.3 1.1 convolution_bitcast_fusion
  304.6 0.8 pad_maximum_fusion.1
  306.1 455.2 %all-reduce.4.cloned.1.call-done = f32[384,128]{1,0:T(8,128)} async-done(((f32[384,128]{1,0:T(8,128)}), f32[384,128]{1,0:T(8,128)}) %all-reduce.4.cloned.1.call-update) | async-done | bytes 196624 | tf_op jit(solution)/shard_map/psum | solution.py:159
  761.3 1.6 slice.816
  762.9 1.5 slice.815
  764.4 1.2 slice_bitcast_fusion
  (600 shorter events, 114.3 us)
Async XLA Ops:
  7.2 284.0 %copy-start = (bf16[125,128]{1,0:T(8,128)(2,1)S(1)}, bf16[125,128]{1,0:T(8,128)(2,1)}, u32[]{:S(2)}) copy-start(bf16[125,128]{1,0:T(8,128)(2,1)} %param.13) | copy-start | bytes 96004
  7.2 28.5 %collective-permute-start = (bf16[12,512]{1,0:T(8,128)(2,1)}, bf16[12,512]{1,0:T(8,128)(2,1)S(1)}, u32[]{:S(2)}, u32[]{:S(2)}) collective-permute-start(bf16[12,512]{1,0:T(8,128)(2,1)} %param.8), channel_id=1, source_target_pairs={{0,32},{32,64},{64,96},{96,128},{128,160},{160,192},{192,224},{224... | collective-permute-start | bytes 36872 | tf_op jit(solution)/shard_map/ppermute | solution.py:16
  11.2 24.4 %collective-permute-start.1 = (bf16[12,512]{1,0:T(8,128)(2,1)}, bf16[12,512]{1,0:T(8,128)(2,1)S(1)}, u32[]{:S(2)}, u32[]{:S(2)}) collective-permute-start(bf16[12,512]{1,0:T(8,128)(2,1)} %param.8), channel_id=1, source_target_pairs={{32,0},{64,32},{96,64},{128,96},{160,128},{192,160},{224,192},{256... | collective-permute-start | bytes 36872 | tf_op jit(solution)/shard_map/ppermute | solution.py:16
  14.6 279.3 %all-to-all-start = ((bf16[32,6,512]{2,1,0:T(8,128)(2,1)}), bf16[32,6,512]{2,1,0:T(8,128)(2,1)S(1)}, u32[]{:S(2)}, u32[]{:S(2)}) async-start(bf16[32,6,512]{2,1,0:T(8,128)(2,1)} %stack.35), calls=%async_computation | async-start | bytes 524288 | tf_op jit(solution)/shard_map/all_to_all | solution.py:119
  33.3 728.0 %all-reduce.4.cloned.1.call-start = ((), (), s32[]{:S(2)}) async-start(), calls=%async_computation.1 | async-start | bytes 393216 | tf_op jit(solution)/shard_map/psum | solution.py:159
  36.4 8.7 %collective-permute-start.2 = (bf16[3,12,512]{2,1,0:T(8,128)(2,1)S(1)}, bf16[3,12,512]{2,1,0:T(8,128)(2,1)S(1)}, u32[]{:S(2)}, u32[]{:S(2)}) collective-permute-start(bf16[3,12,512]{2,1,0:T(8,128)(2,1)S(1)} %get-tuple-element.137), channel_id=1, source_target_pairs={{0,1},{1,2},{2,3},{3,4},{4,5},{5,6},{6,7},{7,8},{8,9},{9,10},{10,1... | collective-permute-start | bytes 110600 | tf_op jit(solution)/shard_map/ppermute | solution.py:16
  39.9 5.7 collective-permute-start.3
  71.3 58.1 %copy-start.153 = (s32[1,2]{1,0:T(1,128)S(1)}, s32[1,2]{1,0:T(1,128)}, u32[]{:S(2)}) copy-start(s32[1,2]{1,0:T(1,128)} %param.12) | copy-start | bytes 28
  167.7 11.7 %copy-start.101 = (bf16[8,8,8,8]{0,3,2,1:T(8,128)(2,1)S(1)}, bf16[8,8,8,8]{0,3,2,1:T(8,128)(2,1)}, u32[]{:S(2)}) copy-start(bf16[8,8,8,8]{0,3,2,1:T(8,128)(2,1)} %get-tuple-element.73) | copy-start | bytes 24580
  168.1 12.3 %copy-start.100 = (bf16[8,8,8,8]{0,3,2,1:T(8,128)(2,1)S(1)}, bf16[8,8,8,8]{0,3,2,1:T(8,128)(2,1)}, u32[]{:S(2)}) copy-start(bf16[8,8,8,8]{0,3,2,1:T(8,128)(2,1)} %get-tuple-element.75) | copy-start | bytes 24580
  169.2 12.3 %copy-start.99 = (bf16[8,8,8,8]{0,3,2,1:T(8,128)(2,1)S(1)}, bf16[8,8,8,8]{0,3,2,1:T(8,128)(2,1)}, u32[]{:S(2)}) copy-start(bf16[8,8,8,8]{0,3,2,1:T(8,128)(2,1)} %get-tuple-element.76) | copy-start | bytes 24580
  170.3 12.3 %copy-start.98 = (bf16[8,8,8,8]{0,3,2,1:T(8,128)(2,1)S(1)}, bf16[8,8,8,8]{0,3,2,1:T(8,128)(2,1)}, u32[]{:S(2)}) copy-start(bf16[8,8,8,8]{0,3,2,1:T(8,128)(2,1)} %get-tuple-element.77) | copy-start | bytes 24580
  171.3 12.3 %copy-start.97 = (bf16[8,8,8,8]{0,3,2,1:T(8,128)(2,1)S(1)}, bf16[8,8,8,8]{0,3,2,1:T(8,128)(2,1)}, u32[]{:S(2)}) copy-start(bf16[8,8,8,8]{0,3,2,1:T(8,128)(2,1)} %get-tuple-element.79) | copy-start | bytes 24580
  172.4 12.3 %copy-start.96 = (bf16[8,8,8,8]{0,3,2,1:T(8,128)(2,1)S(1)}, bf16[8,8,8,8]{0,3,2,1:T(8,128)(2,1)}, u32[]{:S(2)}) copy-start(bf16[8,8,8,8]{0,3,2,1:T(8,128)(2,1)} %get-tuple-element.80) | copy-start | bytes 24580
  173.5 12.3 %copy-start.95 = (bf16[8,8,8,8]{0,3,2,1:T(8,128)(2,1)S(1)}, bf16[8,8,8,8]{0,3,2,1:T(8,128)(2,1)}, u32[]{:S(2)}) copy-start(bf16[8,8,8,8]{0,3,2,1:T(8,128)(2,1)} %get-tuple-element.81) | copy-start | bytes 24580
  174.6 12.3 %copy-start.94 = (bf16[8,8,8,8]{0,3,2,1:T(8,128)(2,1)S(1)}, bf16[8,8,8,8]{0,3,2,1:T(8,128)(2,1)}, u32[]{:S(2)}) copy-start(bf16[8,8,8,8]{0,3,2,1:T(8,128)(2,1)} %get-tuple-element.83) | copy-start | bytes 24580
  175.6 12.3 %copy-start.93 = (bf16[8,8,8,8]{0,3,2,1:T(8,128)(2,1)S(1)}, bf16[8,8,8,8]{0,3,2,1:T(8,128)(2,1)}, u32[]{:S(2)}) copy-start(bf16[8,8,8,8]{0,3,2,1:T(8,128)(2,1)} %get-tuple-element.84) | copy-start | bytes 24580
  180.8 11.6 %copy-start.89 = (bf16[8,8,8,8]{0,3,2,1:T(8,128)(2,1)S(1)}, bf16[8,8,8,8]{0,3,2,1:T(8,128)(2,1)}, u32[]{:S(2)}) copy-start(bf16[8,8,8,8]{0,3,2,1:T(8,128)(2,1)} %get-tuple-element.89) | copy-start | bytes 24580
  181.8 11.6 %copy-start.88 = (bf16[8,8,8,8]{0,3,2,1:T(8,128)(2,1)S(1)}, bf16[8,8,8,8]{0,3,2,1:T(8,128)(2,1)}, u32[]{:S(2)}) copy-start(bf16[8,8,8,8]{0,3,2,1:T(8,128)(2,1)} %get-tuple-element.91) | copy-start | bytes 24580
  182.9 11.6 %copy-start.87 = (bf16[8,8,8,8]{0,3,2,1:T(8,128)(2,1)S(1)}, bf16[8,8,8,8]{0,3,2,1:T(8,128)(2,1)}, u32[]{:S(2)}) copy-start(bf16[8,8,8,8]{0,3,2,1:T(8,128)(2,1)} %get-tuple-element.92) | copy-start | bytes 24580
  184.0 11.6 %copy-start.86 = (bf16[8,8,8,8]{0,3,2,1:T(8,128)(2,1)S(1)}, bf16[8,8,8,8]{0,3,2,1:T(8,128)(2,1)}, u32[]{:S(2)}) copy-start(bf16[8,8,8,8]{0,3,2,1:T(8,128)(2,1)} %get-tuple-element.93) | copy-start | bytes 24580
  185.0 11.6 %copy-start.85 = (bf16[8,8,8,8]{0,3,2,1:T(8,128)(2,1)S(1)}, bf16[8,8,8,8]{0,3,2,1:T(8,128)(2,1)}, u32[]{:S(2)}) copy-start(bf16[8,8,8,8]{0,3,2,1:T(8,128)(2,1)} %get-tuple-element.95) | copy-start | bytes 24580
  186.1 11.6 %copy-start.84 = (bf16[8,8,8,8]{0,3,2,1:T(8,128)(2,1)S(1)}, bf16[8,8,8,8]{0,3,2,1:T(8,128)(2,1)}, u32[]{:S(2)}) copy-start(bf16[8,8,8,8]{0,3,2,1:T(8,128)(2,1)} %get-tuple-element.96) | copy-start | bytes 24580
  187.2 11.6 %copy-start.83 = (bf16[8,8,8,8]{0,3,2,1:T(8,128)(2,1)S(1)}, bf16[8,8,8,8]{0,3,2,1:T(8,128)(2,1)}, u32[]{:S(2)}) copy-start(bf16[8,8,8,8]{0,3,2,1:T(8,128)(2,1)} %get-tuple-element.97) | copy-start | bytes 24580
  188.2 11.6 %copy-start.82 = (bf16[8,8,8,8]{0,3,2,1:T(8,128)(2,1)S(1)}, bf16[8,8,8,8]{0,3,2,1:T(8,128)(2,1)}, u32[]{:S(2)}) copy-start(bf16[8,8,8,8]{0,3,2,1:T(8,128)(2,1)} %get-tuple-element.99) | copy-start | bytes 24580
  189.3 11.6 %copy-start.81 = (bf16[8,8,8,8]{0,3,2,1:T(8,128)(2,1)S(1)}, bf16[8,8,8,8]{0,3,2,1:T(8,128)(2,1)}, u32[]{:S(2)}) copy-start(bf16[8,8,8,8]{0,3,2,1:T(8,128)(2,1)} %get-tuple-element.100) | copy-start | bytes 24580
  190.4 11.6 %copy-start.80 = (bf16[8,8,8,8]{0,3,2,1:T(8,128)(2,1)S(1)}, bf16[8,8,8,8]{0,3,2,1:T(8,128)(2,1)}, u32[]{:S(2)}) copy-start(bf16[8,8,8,8]{0,3,2,1:T(8,128)(2,1)} %get-tuple-element.101) | copy-start | bytes 24580
  191.6 11.5 %copy-start.79 = (bf16[8,8,8,8]{0,3,2,1:T(8,128)(2,1)S(1)}, bf16[8,8,8,8]{0,3,2,1:T(8,128)(2,1)}, u32[]{:S(2)}) copy-start(bf16[8,8,8,8]{0,3,2,1:T(8,128)(2,1)} %get-tuple-element.103) | copy-start | bytes 24580
  192.7 11.5 %copy-start.78 = (bf16[8,8,8,8]{0,3,2,1:T(8,128)(2,1)S(1)}, bf16[8,8,8,8]{0,3,2,1:T(8,128)(2,1)}, u32[]{:S(2)}) copy-start(bf16[8,8,8,8]{0,3,2,1:T(8,128)(2,1)} %get-tuple-element.104) | copy-start | bytes 24580
  193.8 11.5 %copy-start.77 = (bf16[8,8,8,8]{0,3,2,1:T(8,128)(2,1)S(1)}, bf16[8,8,8,8]{0,3,2,1:T(8,128)(2,1)}, u32[]{:S(2)}) copy-start(bf16[8,8,8,8]{0,3,2,1:T(8,128)(2,1)} %get-tuple-element.105) | copy-start | bytes 24580
  194.8 11.5 %copy-start.76 = (bf16[8,8,8,8]{0,3,2,1:T(8,128)(2,1)S(1)}, bf16[8,8,8,8]{0,3,2,1:T(8,128)(2,1)}, u32[]{:S(2)}) copy-start(bf16[8,8,8,8]{0,3,2,1:T(8,128)(2,1)} %get-tuple-element.107) | copy-start | bytes 24580
  195.9 11.5 %copy-start.75 = (bf16[8,8,8,8]{0,3,2,1:T(8,128)(2,1)S(1)}, bf16[8,8,8,8]{0,3,2,1:T(8,128)(2,1)}, u32[]{:S(2)}) copy-start(bf16[8,8,8,8]{0,3,2,1:T(8,128)(2,1)} %get-tuple-element.108) | copy-start | bytes 24580
  197.0 11.5 %copy-start.74 = (bf16[8,8,8,8]{0,3,2,1:T(8,128)(2,1)S(1)}, bf16[8,8,8,8]{0,3,2,1:T(8,128)(2,1)}, u32[]{:S(2)}) copy-start(bf16[8,8,8,8]{0,3,2,1:T(8,128)(2,1)} %get-tuple-element.109) | copy-start | bytes 24580
  198.0 11.5 %copy-start.73 = (bf16[8,8,8,8]{0,3,2,1:T(8,128)(2,1)S(1)}, bf16[8,8,8,8]{0,3,2,1:T(8,128)(2,1)}, u32[]{:S(2)}) copy-start(bf16[8,8,8,8]{0,3,2,1:T(8,128)(2,1)} %get-tuple-element.111) | copy-start | bytes 24580
  199.1 11.4 %copy-start.72 = (bf16[8,8,8,8]{0,3,2,1:T(8,128)(2,1)S(1)}, bf16[8,8,8,8]{0,3,2,1:T(8,128)(2,1)}, u32[]{:S(2)}) copy-start(bf16[8,8,8,8]{0,3,2,1:T(8,128)(2,1)} %get-tuple-element.112) | copy-start | bytes 24580
  200.2 11.5 %copy-start.71 = (bf16[8,8,8,8]{0,3,2,1:T(8,128)(2,1)S(1)}, bf16[8,8,8,8]{0,3,2,1:T(8,128)(2,1)}, u32[]{:S(2)}) copy-start(bf16[8,8,8,8]{0,3,2,1:T(8,128)(2,1)} %get-tuple-element.113) | copy-start | bytes 24580
  201.2 11.5 %copy-start.70 = (bf16[8,8,8,8]{0,3,2,1:T(8,128)(2,1)S(1)}, bf16[8,8,8,8]{0,3,2,1:T(8,128)(2,1)}, u32[]{:S(2)}) copy-start(bf16[8,8,8,8]{0,3,2,1:T(8,128)(2,1)} %get-tuple-element.115) | copy-start | bytes 24580
  202.3 11.4 %copy-start.69 = (bf16[8,8,8,8]{0,3,2,1:T(8,128)(2,1)S(1)}, bf16[8,8,8,8]{0,3,2,1:T(8,128)(2,1)}, u32[]{:S(2)}) copy-start(bf16[8,8,8,8]{0,3,2,1:T(8,128)(2,1)} %get-tuple-element.116) | copy-start | bytes 24580
  203.4 11.4 %copy-start.68 = (bf16[8,8,8,8]{0,3,2,1:T(8,128)(2,1)S(1)}, bf16[8,8,8,8]{0,3,2,1:T(8,128)(2,1)}, u32[]{:S(2)}) copy-start(bf16[8,8,8,8]{0,3,2,1:T(8,128)(2,1)} %get-tuple-element.117) | copy-start | bytes 24580
  204.4 11.5 %copy-start.67 = (bf16[8,8,8,8]{0,3,2,1:T(8,128)(2,1)S(1)}, bf16[8,8,8,8]{0,3,2,1:T(8,128)(2,1)}, u32[]{:S(2)}) copy-start(bf16[8,8,8,8]{0,3,2,1:T(8,128)(2,1)} %get-tuple-element.119) | copy-start | bytes 24580
  205.5 11.5 %copy-start.66 = (bf16[8,8,8,8]{0,3,2,1:T(8,128)(2,1)S(1)}, bf16[8,8,8,8]{0,3,2,1:T(8,128)(2,1)}, u32[]{:S(2)}) copy-start(bf16[8,8,8,8]{0,3,2,1:T(8,128)(2,1)} %get-tuple-element.120) | copy-start | bytes 24580
  206.6 11.5 %copy-start.65 = (bf16[8,8,8,8]{0,3,2,1:T(8,128)(2,1)S(1)}, bf16[8,8,8,8]{0,3,2,1:T(8,128)(2,1)}, u32[]{:S(2)}) copy-start(bf16[8,8,8,8]{0,3,2,1:T(8,128)(2,1)} %get-tuple-element.121) | copy-start | bytes 24580
  207.6 11.5 %copy-start.64 = (bf16[8,8,8,8]{0,3,2,1:T(8,128)(2,1)S(1)}, bf16[8,8,8,8]{0,3,2,1:T(8,128)(2,1)}, u32[]{:S(2)}) copy-start(bf16[8,8,8,8]{0,3,2,1:T(8,128)(2,1)} %get-tuple-element.123) | copy-start | bytes 24580
  208.7 11.5 %copy-start.63 = (bf16[8,8,8,8]{0,3,2,1:T(8,128)(2,1)S(1)}, bf16[8,8,8,8]{0,3,2,1:T(8,128)(2,1)}, u32[]{:S(2)}) copy-start(bf16[8,8,8,8]{0,3,2,1:T(8,128)(2,1)} %get-tuple-element.124) | copy-start | bytes 24580
  210.8 11.4 %copy-start.61 = (bf16[8,8,8,8]{0,3,2,1:T(8,128)(2,1)S(1)}, bf16[8,8,8,8]{0,3,2,1:T(8,128)(2,1)}, u32[]{:S(2)}) copy-start(bf16[8,8,8,8]{0,3,2,1:T(8,128)(2,1)} %get-tuple-element.127) | copy-start | bytes 24580
  213.0 11.5 %copy-start.59 = (bf16[8,8,8,8]{0,3,2,1:T(8,128)(2,1)S(1)}, bf16[8,8,8,8]{0,3,2,1:T(8,128)(2,1)}, u32[]{:S(2)}) copy-start(bf16[8,8,8,8]{0,3,2,1:T(8,128)(2,1)} %get-tuple-element.129) | copy-start | bytes 24580
  214.0 11.4 %copy-start.58 = (bf16[8,8,8,8]{0,3,2,1:T(8,128)(2,1)S(1)}, bf16[8,8,8,8]{0,3,2,1:T(8,128)(2,1)}, u32[]{:S(2)}) copy-start(bf16[8,8,8,8]{0,3,2,1:T(8,128)(2,1)} %get-tuple-element.131) | copy-start | bytes 24580
  215.1 11.5 %copy-start.57 = (bf16[8,8,8,8]{0,3,2,1:T(8,128)(2,1)S(1)}, bf16[8,8,8,8]{0,3,2,1:T(8,128)(2,1)}, u32[]{:S(2)}) copy-start(bf16[8,8,8,8]{0,3,2,1:T(8,128)(2,1)} %get-tuple-element.132) | copy-start | bytes 24580
  216.2 11.8 %copy-start.56 = (bf16[8,8,8,8]{0,3,2,1:T(8,128)(2,1)S(1)}, bf16[8,8,8,8]{0,3,2,1:T(8,128)(2,1)}, u32[]{:S(2)}) copy-start(bf16[8,8,8,8]{0,3,2,1:T(8,128)(2,1)} %get-tuple-element.133) | copy-start | bytes 24580
  217.2 11.8 %copy-start.55 = (bf16[8,8,8,8]{0,3,2,1:T(8,128)(2,1)S(1)}, bf16[8,8,8,8]{0,3,2,1:T(8,128)(2,1)}, u32[]{:S(2)}) copy-start(bf16[8,8,8,8]{0,3,2,1:T(8,128)(2,1)} %get-tuple-element.130) | copy-start | bytes 24580
  218.3 11.8 %copy-start.54 = (bf16[8,8,8,8]{0,3,2,1:T(8,128)(2,1)S(1)}, bf16[8,8,8,8]{0,3,2,1:T(8,128)(2,1)}, u32[]{:S(2)}) copy-start(bf16[8,8,8,8]{0,3,2,1:T(8,128)(2,1)} %get-tuple-element.126) | copy-start | bytes 24580
  219.4 11.8 %copy-start.53 = (bf16[8,8,8,8]{0,3,2,1:T(8,128)(2,1)S(1)}, bf16[8,8,8,8]{0,3,2,1:T(8,128)(2,1)}, u32[]{:S(2)}) copy-start(bf16[8,8,8,8]{0,3,2,1:T(8,128)(2,1)} %get-tuple-element.122) | copy-start | bytes 24580
  220.4 11.8 %copy-start.52 = (bf16[8,8,8,8]{0,3,2,1:T(8,128)(2,1)S(1)}, bf16[8,8,8,8]{0,3,2,1:T(8,128)(2,1)}, u32[]{:S(2)}) copy-start(bf16[8,8,8,8]{0,3,2,1:T(8,128)(2,1)} %get-tuple-element.118) | copy-start | bytes 24580
  221.5 11.8 %copy-start.51 = (bf16[8,8,8,8]{0,3,2,1:T(8,128)(2,1)S(1)}, bf16[8,8,8,8]{0,3,2,1:T(8,128)(2,1)}, u32[]{:S(2)}) copy-start(bf16[8,8,8,8]{0,3,2,1:T(8,128)(2,1)} %get-tuple-element.114) | copy-start | bytes 24580
  222.6 11.8 %copy-start.50 = (bf16[8,8,8,8]{0,3,2,1:T(8,128)(2,1)S(1)}, bf16[8,8,8,8]{0,3,2,1:T(8,128)(2,1)}, u32[]{:S(2)}) copy-start(bf16[8,8,8,8]{0,3,2,1:T(8,128)(2,1)} %get-tuple-element.110) | copy-start | bytes 24580
  223.6 11.8 %copy-start.49 = (bf16[8,8,8,8]{0,3,2,1:T(8,128)(2,1)S(1)}, bf16[8,8,8,8]{0,3,2,1:T(8,128)(2,1)}, u32[]{:S(2)}) copy-start(bf16[8,8,8,8]{0,3,2,1:T(8,128)(2,1)} %get-tuple-element.106) | copy-start | bytes 24580
  224.7 11.8 %copy-start.48 = (bf16[8,8,8,8]{0,3,2,1:T(8,128)(2,1)S(1)}, bf16[8,8,8,8]{0,3,2,1:T(8,128)(2,1)}, u32[]{:S(2)}) copy-start(bf16[8,8,8,8]{0,3,2,1:T(8,128)(2,1)} %get-tuple-element.102) | copy-start | bytes 24580
  225.8 11.8 %copy-start.47 = (bf16[8,8,8,8]{0,3,2,1:T(8,128)(2,1)S(1)}, bf16[8,8,8,8]{0,3,2,1:T(8,128)(2,1)}, u32[]{:S(2)}) copy-start(bf16[8,8,8,8]{0,3,2,1:T(8,128)(2,1)} %get-tuple-element.98) | copy-start | bytes 24580
  226.9 11.8 %copy-start.46 = (bf16[8,8,8,8]{0,3,2,1:T(8,128)(2,1)S(1)}, bf16[8,8,8,8]{0,3,2,1:T(8,128)(2,1)}, u32[]{:S(2)}) copy-start(bf16[8,8,8,8]{0,3,2,1:T(8,128)(2,1)} %get-tuple-element.94) | copy-start | bytes 24580
  240.0 14.1 %copy-start.45 = (bf16[8,8,8,8]{0,3,2,1:T(8,128)(2,1)S(1)}, bf16[8,8,8,8]{0,3,2,1:T(8,128)(2,1)}, u32[]{:S(2)}) copy-start(bf16[8,8,8,8]{0,3,2,1:T(8,128)(2,1)} %get-tuple-element.58) | copy-start | bytes 24580
  241.1 13.5 %copy-start.44 = (bf16[8,8,8,8]{0,3,2,1:T(8,128)(2,1)S(1)}, bf16[8,8,8,8]{0,3,2,1:T(8,128)(2,1)}, u32[]{:S(2)}) copy-start(bf16[8,8,8,8]{0,3,2,1:T(8,128)(2,1)} %get-tuple-element.55) | copy-start | bytes 24580
  242.2 12.9 %copy-start.42 = (bf16[8,8,8,8]{0,3,2,1:T(8,128)(2,1)S(1)}, bf16[8,8,8,8]{0,3,2,1:T(8,128)(2,1)}, u32[]{:S(2)}) copy-start(bf16[8,8,8,8]{0,3,2,1:T(8,128)(2,1)} %get-tuple-element.56) | copy-start | bytes 24580
  243.2 12.3 %copy-start.41 = (bf16[8,8,8,8]{0,3,2,1:T(8,128)(2,1)S(1)}, bf16[8,8,8,8]{0,3,2,1:T(8,128)(2,1)}, u32[]{:S(2)}) copy-start(bf16[8,8,8,8]{0,3,2,1:T(8,128)(2,1)} %get-tuple-element.57) | copy-start | bytes 24580
  244.3 11.7 %copy-start.40 = (bf16[8,8,8,8]{0,3,2,1:T(8,128)(2,1)S(1)}, bf16[8,8,8,8]{0,3,2,1:T(8,128)(2,1)}, u32[]{:S(2)}) copy-start(bf16[8,8,8,8]{0,3,2,1:T(8,128)(2,1)} %get-tuple-element.54) | copy-start | bytes 24580
  (98 other events, 642.5 us)
Sparse Core Ops, SparseCore 0:
  305.6 455.6 all-reduce.3
